TPU v7x, 128 devices: a whole 4x4x4 slice. The times are simulated.
128 devices in a mesh: freq: 8 (over x, core), bl: 16 (over z, y).
Axes of the slice: x: 4, y: 4, z: 4, core: 2. Of those that a mesh axis runs over, the one named last changes fastest.
Arguments:
- coherency: bfloat16 [8, 1024, 8192], P(None, 'bl', 'freq'), may hold values from -2 to 2
- visibility: float32 [8, 1024, 256], P(None, 'bl', 'freq'), may hold values from -6 to 6
- span_lengths: int32 [1024], P('bl'), may hold values from 1 to 8, 4096 in all
- station_pairs: int32 [2, 1024], P(None, 'bl'), may hold values from 0 to 61, as said below
- jones_field: float32 [8, 64, 8192], P(None, 'bl', 'freq'), may hold values from -1.2 to 2.2
- dual_field: float32 [8, 64, 8192], P(None, 'bl', 'freq'), may hold values from -6 to 6
- consensus_coeffs: float32 [4, 8, 64, 32], P(None, None, 'bl'), may hold values from -6 to 6
Outputs:
- jones_next: float32 [8, 64, 8192], P(None, 'bl', 'freq')
- dual_next: float32 [8, 64, 8192], P(None, 'bl', 'freq')
- consensus_next: float32 [4, 8, 64, 32], P(None, None, 'bl')
Inputs may be any that keep to these rules, and one draw needn't show every extreme that they name: `station_pairs`: the two stations of a row differ; station numbers stay under 62.
All inputs are finite; a program needn't handle non-finite values. No bound on the sum of `span_lengths` on one device may be relied on, other than what follows from the above.
Results may differ from a plain program's by a relative error of at most 0.0003.
Values sent between devices are 32-bit elements; how exact they have to be, the bound alone decides.
A program may use at most 64 MiB of HBM per device.

v0:
```python
import functools

import jax
import jax.numpy as jnp
import numpy as np
from jax import lax
from jax.experimental import pallas as pl
from jax.experimental.pallas import tpu as pltpu
from jax.sharding import PartitionSpec as P

CHANS = 256
ITERS = 2
NTERMS = 4
PENALTY = 4.0
DAMPING = 0.5

RING = 4
PEERS = 16
FREQS = 8
STAGES = 2
QUARTERS = 4
BAND = 16
DIRS = 32
SLOTS = 64
ROWS = PEERS * BAND
HEAD = 24
GROUP = 4

MESH = pl.DeviceIdType.MESH
F32 = jnp.float32
BF16 = jnp.bfloat16


def basis_table():
    channel = np.arange(CHANS, dtype=np.float64) + 0.5
    order = np.arange(NTERMS, dtype=np.float64)
    return np.cos(np.pi * order[:, None] * channel[None, :] / CHANS).astype(np.float32)


def norm_of(term):
    return float(CHANS) if term == 0 else 0.5 * CHANS


def product(a, b):
    real, imag = [], []
    for i in range(2):
        for j in range(2):
            real.append(
                a[2 * i] * b[j]
                + a[2 * i + 1] * b[2 + j]
                - a[4 + 2 * i] * b[4 + j]
                - a[4 + 2 * i + 1] * b[4 + 2 + j]
            )
            imag.append(
                a[2 * i] * b[4 + j]
                + a[2 * i + 1] * b[4 + 2 + j]
                + a[4 + 2 * i] * b[j]
                + a[4 + 2 * i + 1] * b[2 + j]
            )
    return real + imag


def product_adjoint(a, b):
    real, imag = [], []
    for i in range(2):
        for j in range(2):
            real.append(
                a[2 * i] * b[2 * j]
                + a[2 * i + 1] * b[2 * j + 1]
                + a[4 + 2 * i] * b[4 + 2 * j]
                + a[4 + 2 * i + 1] * b[4 + 2 * j + 1]
            )
            imag.append(
                a[4 + 2 * i] * b[2 * j]
                + a[4 + 2 * i + 1] * b[2 * j + 1]
                - a[2 * i] * b[4 + 2 * j]
                - a[2 * i + 1] * b[4 + 2 * j + 1]
            )
    return real + imag


def adjoint_product(a, b):
    real, imag = [], []
    for i in range(2):
        for j in range(2):
            real.append(
                a[i] * b[j] + a[2 + i] * b[2 + j] + a[4 + i] * b[4 + j] + a[6 + i] * b[6 + j]
            )
            imag.append(
                a[i] * b[4 + j] + a[2 + i] * b[6 + j] - a[4 + i] * b[j] - a[6 + i] * b[2 + j]
            )
    return real + imag


def square_right(a):
    top = a[0] * a[0] + a[1] * a[1] + a[4] * a[4] + a[5] * a[5]
    bottom = a[2] * a[2] + a[3] * a[3] + a[6] * a[6] + a[7] * a[7]
    real = a[0] * a[2] + a[4] * a[6] + a[1] * a[3] + a[5] * a[7]
    imag = a[4] * a[2] - a[0] * a[6] + a[5] * a[3] - a[1] * a[7]
    return [top, bottom, real, imag]


def square_left(a):
    return square_right([a[0], a[2], a[1], a[3], -a[4], -a[6], -a[5], -a[7]])


def halves(x):
    high = x.astype(BF16)
    return high, (x - high.astype(F32)).astype(BF16)


def lane_block(shape):
    return lax.shift_right_logical(lax.broadcasted_iota(jnp.int32, shape, len(shape) - 1), 5)


def swap_blocks(x):
    block = lane_block(x[0].shape)
    left = block < 2
    even = (block & 1) == 0
    halfway = [None] * 4
    for low in range(2):
        first, second = x[low], x[2 + low]
        halfway[low] = jnp.where(left, first, pltpu.roll(second, 64, 1))
        halfway[2 + low] = jnp.where(left, pltpu.roll(first, 64, 1), second)
    out = [None] * 4
    for high in range(2):
        first, second = halfway[2 * high], halfway[2 * high + 1]
        out[2 * high] = jnp.where(even, first, pltpu.roll(second, 32, 1))
        out[2 * high + 1] = jnp.where(even, pltpu.roll(first, 96, 1), second)
    return out


def spread_lanes(x):
    x = x + pltpu.roll(x, 64, 1)
    return x + pltpu.roll(x, 32, 1)


def dot(a, b):
    return jnp.dot(a, b, preferred_element_type=F32)


def kernel(
    basis, coh, vis, span, pairs, jones, dual, cons,
    jones_out, dual_out, cons_out,
    csend, crecv, hsend, hrecv, rsend, rrecv, psend, precv,
    meta, const, dual_t, jpq, vis_x, terms, ohg, ohs, jrhs, ones_blk, field, prior,
    csend_sem, crecv_sem, hsend_sem, hrecv_sem, rsend_sem, rrecv_sem, psend_sem, precv_sem, own_sem,
):
    me = lax.axis_index("bl")
    fr = lax.axis_index("freq")
    z, y = me // RING, me % RING
    first_chan = fr * (CHANS // FREQS)

    def ahead(j):
        return lax.rem(z + j // RING, RING) * RING + lax.rem(y + j % RING, RING)

    def behind(j):
        return lax.rem(z + RING - j // RING, RING) * RING + lax.rem(y + RING - j % RING, RING)

    def freq_ahead(g):
        return lax.rem(fr + g, FREQS)

    barrier = pltpu.get_barrier_semaphore()
    for j in range(1, PEERS):
        pl.semaphore_signal(barrier, inc=1, device_id={"bl": ahead(j)}, device_id_type=MESH)
    for g in range(1, FREQS):
        pl.semaphore_signal(barrier, inc=1, device_id={"freq": freq_ahead(g)}, device_id_type=MESH)

    def basis_at(term, chan):
        return basis[term, first_chan + chan]


    def c_copy(t, j):
        return pltpu.make_async_remote_copy(
            src_ref=csend.at[t, ahead(j)], dst_ref=crecv.at[t, j],
            send_sem=csend_sem.at[t, j], recv_sem=crecv_sem.at[t, j],
            device_id={"bl": ahead(j)}, device_id_type=MESH,
        )

    def h_copy(t, j):
        return pltpu.make_async_remote_copy(
            src_ref=hsend.at[t, ahead(j)], dst_ref=hrecv.at[t, j],
            send_sem=hsend_sem.at[t, j], recv_sem=hrecv_sem.at[t, j],
            device_id={"bl": ahead(j)}, device_id_type=MESH,
        )

    def r_copy(t, j):
        return pltpu.make_async_remote_copy(
            src_ref=rsend.at[t, j], dst_ref=rrecv.at[t, me],
            send_sem=rsend_sem.at[t, j], recv_sem=rrecv_sem.at[t, j],
            device_id={"bl": behind(j)}, device_id_type=MESH,
        )

    def p_copy(g):
        return pltpu.make_async_remote_copy(
            src_ref=psend, dst_ref=precv.at[fr],
            send_sem=psend_sem.at[g], recv_sem=precv_sem.at[g],
            device_id={"freq": freq_ahead(g)}, device_id_type=MESH,
        )


    for m in range(NTERMS):
        for s in range(4):
            const[m, :, DIRS * s : DIRS * s + DIRS] = cons[m, :, s, :]
    meta[...] = jnp.zeros_like(meta)
    meta[0:2, 0:64] = pairs[...].astype(F32)
    meta[2:3, 0:64] = span[...].astype(F32)
    vis_t = jnp.transpose(vis[...].reshape(8 * 64, 32))
    for t in range(STAGES):
        for d in range(PEERS):
            for i in range(4):
                hsend[t, d, 16 + i : 17 + i, :] = vis_t[
                    PEERS * t + d : PEERS * t + d + 1, 128 * i : 128 * i + 128
                ]
            hsend[t, d, 20:24, :] = meta[0:4, :]

    def build_head(t):
        for tile in range(4):
            lanes = pl.ds(128 * (4 * t + tile), 128)
            j_tile = swap_blocks([jones[:, s, lanes] for s in range(4)])
            d_tile = swap_blocks([dual[:, s, lanes] for s in range(4)])
            for a in range(4):
                d = 4 * tile + a
                chan = PEERS * t + d
                smooth = const[0] * basis_at(0, chan)
                for m in range(1, NTERMS):
                    smooth = smooth + const[m] * basis_at(m, chan)
                dual_t[chan] = d_tile[a]
                hsend[t, d, 0:8, :] = j_tile[a]
                hsend[t, d, 8:16, :] = PENALTY * smooth - d_tile[a]

    def build_c(t):
        def one(c, _):
            for tile in range(4):
                lanes = pl.ds(128 * (4 * t + tile), 128)
                parts = swap_blocks(
                    [coh[c, BAND * q : BAND * q + BAND, lanes].astype(F32) for q in range(QUARTERS)]
                )
                for a in range(4):
                    csend[t, 4 * tile + a, c] = parts[a]
            return 0

        lax.fori_loop(0, 8, one, 0)

    def own_copies(t):
        return (
            pltpu.make_async_copy(hsend.at[t, me], hrecv.at[t, 0], own_sem.at[2 * t]),
            pltpu.make_async_copy(csend.at[t, me], crecv.at[t, 0], own_sem.at[2 * t + 1]),
        )

    def send_all(t):
        for copy in own_copies(t):
            copy.start()

        def head(j, _):
            h_copy(t, j).start()
            return 0

        def body(j, _):
            c_copy(t, j).start()
            return 0

        lax.fori_loop(1, PEERS, head, 0)
        lax.fori_loop(1, PEERS, body, 0)

    build_head(0)
    build_c(0)
    pl.semaphore_wait(barrier, PEERS - 1 + FREQS - 1)
    send_all(0)
    build_head(1)
    build_c(1)
    send_all(1)

    row_block = lax.shift_right_logical(lax.broadcasted_iota(jnp.int32, (256, 128), 0), 5) & 3
    ones_blk[...] = jnp.where(row_block == lane_block((256, 128)), 1.0, 0.0).astype(BF16)

    band_mask = (lax.broadcasted_iota(jnp.int32, (BAND, 128), 1) & (BAND - 1)) == (
        lax.broadcasted_iota(jnp.int32, (BAND, 128), 0)
    )

    def banded(t, row):
        return jnp.concatenate(
            [
                jnp.where(band_mask, jnp.broadcast_to(hrecv[t, j, row : row + 1, :], (BAND, 128)), 0.0)
                for j in range(PEERS)
            ],
            axis=0,
        )

    def build_onehots():
        source = lax.broadcasted_iota(jnp.int32, (128, 256), 0)
        target = lax.broadcasted_iota(jnp.int32, (128, 256), 1)
        expand = jnp.where(
            lax.shift_right_logical(source, 4) == lax.shift_right_logical(target, 6), 1.0, 0.0
        ).astype(BF16)
        position = lax.broadcasted_iota(jnp.int32, (1, 256), 1) & (SLOTS - 1)
        j = position & (PEERS - 1)
        owner_z = (z + RING - lax.shift_right_logical(j, 2)) & (RING - 1)
        owner_y = (y + RING - (j & 3)) & (RING - 1)
        label = 4 * (owner_z * RING + owner_y) + lax.shift_right_logical(position, 4)
        label = label.astype(F32)
        weight = dot(banded(0, 22).astype(BF16), expand)
        for side in range(2):
            station = dot(banded(0, 20 + side).astype(BF16), expand)
            hit = station == label
            onehot = jnp.where(hit, 1.0, 0.0).astype(BF16)
            ohg[ROWS * side : ROWS * side + ROWS, 0:256] = onehot
            ohg[ROWS * side : ROWS * side + ROWS, 256:512] = onehot
            weighted = jnp.transpose(jnp.where(hit, weight, 0.0)).astype(BF16)
            ohs[:, 512 * side : 512 * side + 256] = weighted
            ohs[:, 512 * side + 256 : 512 * side + 512] = weighted

    def build_visibility(t):
        source = lax.broadcasted_iota(jnp.int32, (256, 256), 0) & 127
        target = lax.broadcasted_iota(jnp.int32, (256, 256), 1)
        expand = jnp.where(
            lax.shift_right_logical(source, 4) == lax.shift_right_logical(target, 5), 1.0, 0.0
        ).astype(BF16)
        for i in range(4):
            high, low = halves(banded(t, 16 + i))
            out = dot(jnp.concatenate([high, low], axis=1), expand)
            vis_x[2 * i] = out[:, 0:128]
            vis_x[2 * i + 1] = out[:, 128:256]

    def build_field(t):
        block = lane_block((PEERS, 128))
        for c in range(16):
            flat = jnp.concatenate([hrecv[t, j, c : c + 1, :] for j in range(PEERS)], axis=0)
            target = field if c < 8 else prior
            for s in range(4):
                target[c % 8, PEERS * s : PEERS * s + PEERS] = spread_lanes(
                    jnp.where(block == s, flat, 0.0)
                )

    def gather():
        block = lane_block((SLOTS, 128))
        for c in range(8):
            for at, part in enumerate(halves(field[c])):
                for q in range(QUARTERS):
                    first = 256 * at + SLOTS * q
                    jrhs[first : first + SLOTS, 128 * c : 128 * c + 128] = jnp.where(
                        block == q, part.astype(F32), 0.0
                    ).astype(BF16)
        for c in range(4):
            jpq[:, 256 * c : 256 * c + 256] = dot(ohg[...], jrhs[:, 256 * c : 256 * c + 256])

    def process(t, group):
        size = GROUP * BAND
        first = pl.multiple_of(group * size, size)
        rows = pl.ds(first, size)
        sources = pl.ds(group * GROUP, GROUP)
        coherent = [crecv[t, sources, c].reshape(size, 128) for c in range(8)]
        left = [jpq[rows, 128 * c : 128 * c + 128] for c in range(8)]
        right = [jpq[pl.ds(ROWS + first, size), 128 * c : 128 * c + 128] for c in range(8)]
        applied = product_adjoint(coherent, right)
        model = product(left, applied)
        outer = product(left, coherent)
        split = [jnp.concatenate(halves(x), axis=1) for x in model]
        total = dot(jnp.concatenate(split, axis=0), ones_blk[...])
        misfit = [vis_x[c, rows, :] - total[size * c : size * c + size] for c in range(8)]
        for side in range(2):
            if side == 0:
                out = product_adjoint(misfit, applied) + square_right(applied)
            else:
                out = adjoint_product(misfit, outer) + square_left(outer)
            for c in range(12):
                for at, part in enumerate(halves(out[c])):
                    terms[pl.ds(ROWS * (2 * side + at) + first, size), 128 * c : 128 * c + 128] = part

    def solve():
        block = lane_block((SLOTS, 128))
        sums = []
        for pair in range(6):
            res = dot(ohs[...], terms[:, 256 * pair : 256 * pair + 256])
            for half in range(2):
                part = res[:, 128 * half : 128 * half + 128]
                total = jnp.where(block == 0, part[0:SLOTS], 0.0)
                for q in range(1, QUARTERS):
                    total = jnp.where(block == q, part[SLOTS * q : SLOTS * q + SLOTS], total)
                sums.append(spread_lanes(total))
        current = [field[c] for c in range(8)]
        rhs = [sums[c] + prior[c] - PENALTY * current[c] for c in range(8)]
        top = sums[8] + PENALTY
        bottom = sums[9] + PENALTY
        real, imag = sums[10], sums[11]
        scale = DAMPING / (top * bottom - real * real - imag * imag)
        for i in range(2):
            a, b = rhs[2 * i], rhs[2 * i + 1]
            c, d = rhs[4 + 2 * i], rhs[4 + 2 * i + 1]
            field[2 * i] = current[2 * i] + scale * (a * bottom - b * real - d * imag)
            field[2 * i + 1] = current[2 * i + 1] + scale * (b * top - a * real + c * imag)
            field[4 + 2 * i] = current[4 + 2 * i] + scale * (c * bottom - d * real + b * imag)
            field[5 + 2 * i] = current[5 + 2 * i] + scale * (d * top - c * real - a * imag)

    def send_back(t):
        block = lane_block((PEERS, 128))
        for c in range(8):
            whole = field[c]
            flat = jnp.where(block == 0, whole[0:PEERS], 0.0)
            for s in range(1, 4):
                flat = jnp.where(block == s, whole[PEERS * s : PEERS * s + PEERS], flat)
            for j in range(PEERS):
                rsend[t, j, c : c + 1, :] = flat[j : j + 1]
        rrecv[t, me] = rsend[t, 0]
        for j in range(1, PEERS):
            r_copy(t, j).start()

    def wait_each(copy, t):
        def one(j, _):
            copy(t, j).wait()
            return 0

        lax.fori_loop(1, PEERS, one, 0)

    for t in range(STAGES):
        own = own_copies(t)
        own[0].wait()
        wait_each(h_copy, t)
        if t == 0:
            build_onehots()
        build_visibility(t)
        build_field(t)
        gather()
        own[1].wait()

        def first_sweep(group, _):
            def arrive(j, _):
                c_copy(t, j).wait()
                return 0

            lax.fori_loop(jnp.maximum(group * GROUP, 1), (group + 1) * GROUP, arrive, 0)
            process(t, group)
            return 0

        def later_sweep(group, _):
            process(t, group)
            return 0

        lax.fori_loop(0, PEERS // GROUP, first_sweep, 0)
        solve()
        for _ in range(1, ITERS):
            gather()
            lax.fori_loop(0, PEERS // GROUP, later_sweep, 0)
            solve()
        send_back(t)

    projected = [jnp.zeros((8, 128), F32) for _ in range(NTERMS)]
    for t in range(STAGES):
        wait_each(r_copy, t)
        for d in range(PEERS):
            chan = PEERS * t + d
            blended = rrecv[t, d] + dual_t[chan] * (1.0 / PENALTY)
            for m in range(NTERMS):
                projected[m] = projected[m] + blended * (basis_at(m, chan) * (1.0 / norm_of(m)))
    for m in range(NTERMS):
        psend[m] = projected[m]
        precv[fr, m] = projected[m]
    for g in range(1, FREQS):
        p_copy(g).start()
    for t in range(STAGES):
        for tile in range(4):
            lanes = pl.ds(128 * (4 * t + tile), 128)
            parts = swap_blocks([rrecv[t, 4 * tile + a] for a in range(4)])
            for s in range(4):
                jones_out[:, s, lanes] = parts[s]
    for g in range(1, FREQS):
        p_copy(g).wait()
    block = lane_block((8, 128))
    smooth = []
    for m in range(NTERMS):
        total = precv[0, m]
        for g in range(1, FREQS):
            total = total + precv[g, m]
        for s in range(4):
            cons_out[m, :, s, :] = total[:, DIRS * s : DIRS * s + DIRS]
        smooth.append([spread_lanes(jnp.where(block == s, total, 0.0)) for s in range(4)])
    lane = lane_block((1, 128))
    for tile in range(8):
        lanes = pl.ds(128 * tile, 128)
        rows = []
        for m in range(NTERMS):
            row = jnp.full((1, 128), basis_at(m, 4 * tile), F32)
            for a in range(1, 4):
                row = jnp.where(lane == a, basis_at(m, 4 * tile + a), row)
            rows.append(row)
        for s in range(4):
            fitted = rows[0] * smooth[0][s]
            for m in range(1, NTERMS):
                fitted = fitted + rows[m] * smooth[m][s]
            dual_out[:, s, lanes] = dual[:, s, lanes] + PENALTY * (jones_out[:, s, lanes] - fitted)


def shards(coherency, visibility, span_lengths, station_pairs, jones_field, dual_field, consensus):
    vmem = pl.BlockSpec(memory_space=pltpu.VMEM)
    smem = pl.BlockSpec(memory_space=pltpu.SMEM)
    dma = pltpu.SemaphoreType.DMA
    return pl.pallas_call(
        kernel,
        out_shape=(
            jax.ShapeDtypeStruct(jones_field.shape, F32),
            jax.ShapeDtypeStruct(dual_field.shape, F32),
            jax.ShapeDtypeStruct(consensus.shape, F32),
        ),
        in_specs=[smem] + [vmem] * 7,
        out_specs=(vmem,) * 3,
        scratch_shapes=[
            pltpu.VMEM((STAGES, PEERS, 8, BAND, 128), F32),
            pltpu.VMEM((STAGES, PEERS, 8, BAND, 128), F32),
            pltpu.VMEM((STAGES, PEERS, HEAD, 128), F32),
            pltpu.VMEM((STAGES, PEERS, HEAD, 128), F32),
            pltpu.VMEM((STAGES, PEERS, 8, 128), F32),
            pltpu.VMEM((STAGES, PEERS, 8, 128), F32),
            pltpu.VMEM((NTERMS, 8, 128), F32),
            pltpu.VMEM((FREQS, NTERMS, 8, 128), F32),
            pltpu.VMEM((8, 128), F32),
            pltpu.VMEM((NTERMS, 8, 128), F32),
            pltpu.VMEM((STAGES * PEERS, 8, 128), F32),
            pltpu.VMEM((2 * ROWS, 8 * 128), F32),
            pltpu.VMEM((8, ROWS, 128), F32),
            pltpu.VMEM((4 * ROWS, 12 * 128), BF16),
            pltpu.VMEM((2 * ROWS, 512), BF16),
            pltpu.VMEM((QUARTERS * SLOTS, 4 * ROWS), BF16),
            pltpu.VMEM((2 * QUARTERS * SLOTS, 8 * 128), BF16),
            pltpu.VMEM((256, 128), BF16),
            pltpu.VMEM((8, SLOTS, 128), F32),
            pltpu.VMEM((8, SLOTS, 128), F32),
            dma((STAGES, PEERS)),
            dma((STAGES, PEERS)),
            dma((STAGES, PEERS)),
            dma((STAGES, PEERS)),
            dma((STAGES, PEERS)),
            dma((STAGES, PEERS)),
            dma((FREQS,)),
            dma((FREQS,)),
            dma((2 * STAGES,)),
        ],
        compiler_params=pltpu.CompilerParams(
            collective_id=0, has_side_effects=True, vmem_limit_bytes=40 * 2**20
        ),
        name="calibrate",
    )(
        jnp.asarray(basis_table()),
        coherency,
        visibility,
        span_lengths.reshape(1, -1),
        station_pairs,
        jones_field,
        dual_field,
        consensus,
    )


def solution(mesh):
    in_specs = (
        P(None, "bl", "freq"),
        P(None, "bl", "freq"),
        P("bl"),
        P(None, "bl"),
        P(None, "bl", "freq"),
        P(None, "bl", "freq"),
        P(None, None, "bl", None),
    )
    out_specs = (P(None, "bl", "freq"), P(None, "bl", "freq"), P(None, None, "bl", None))
    return jax.shard_map(shards, mesh=mesh, in_specs=in_specs, out_specs=out_specs, check_vma=False)
```

profile of v0, /device:TPU:1, one launch (start us, length us, event | category | flops | bytes accessed | tf_op | source)
XLA Modules:
  0.0 65.4 jit_solution(86718849496820230)
XLA Ops:
  0.6 0.0 copy-start.1
  0.6 0.0 copy-start.2
  0.7 0.0 copy-start.3
  0.7 0.0 copy-start.4
  0.7 0.0 copy-start.5
  0.7 0.0 copy-start.6
  0.7 1.1 %copy.11.vis = f32[8,64,32]{2,1,0:T(8,128)S(1)} copy(f32[8,64,32]{1,2,0:T(8,128)} %param.9) | data formatting | bytes 131072 | tf_op args[1]
  1.8 0.0 copy-done.1
  1.8 0.0 copy-done.2
  1.8 0.0 copy-done.3
  1.9 0.0 copy-done.4
  1.9 0.0 copy-done.5
  1.9 0.0 copy-done.6
  1.9 0.0 copy-start
  1.9 1.2 %copy-done = bf16[8,64,1024]{2,1,0:T(8,128)(2,1)S(1)} copy-done((bf16[8,64,1024]{2,1,0:T(8,128)(2,1)S(1)}, bf16[8,64,1024]{2,1,0:T(8,128)(2,1)}, u32[]{:S(2)}) %copy-start) | copy-done | bytes 1048600
  3.1 60.3 %calibrate.1 = (f32[8,4,1024]{2,1,0:T(4,128)S(1)}, f32[8,4,1024]{2,1,0:T(4,128)S(1)}, f32[4,8,4,32]{3,2,1,0:T(4,128)S(1)}) custom-call(f32[4,256]{1,0:T(4,128)S(1)} %copy-done.4, bf16[8,64,1024]{2,1,0:T(8,128)(2,1)S(1)} %copy-done, f32[8,64,32]{2,1,0:T(8,128)S(1)} %copy.11.vis, s32[1,64]{1,0:T(1,128)S(1)} %bitcast.1, s32[2,64]{1,0:T(2,128)S(1)} %copy-done.5, ...), custom_call_target="tpu_custom_call" | custom-call | tf_op jit(solution)/shard_map/calibrate/pallas_call | solution.py:497
  63.5 0.7 %copy.15 = f32[8,4,1024]{2,1,0:T(4,128)} copy(f32[8,4,1024]{2,1,0:T(4,128)S(1)} %get-tuple-element.6) | data formatting | bytes 262144
  64.1 0.7 %copy.16 = f32[8,4,1024]{2,1,0:T(4,128)} copy(f32[8,4,1024]{2,1,0:T(4,128)S(1)} %get-tuple-element.7) | data formatting | bytes 262144
  64.8 0.6 copy.17
Async XLA Ops:
  0.6 1.2 %copy-start.1 = (f32[8,4,1024]{2,1,0:T(4,128)S(1)}, f32[8,4,1024]{2,1,0:T(4,128)}, u32[]{:S(2)}) copy-start(f32[8,4,1024]{2,1,0:T(4,128)} %jones.1) | copy-start | bytes 393220
  0.6 1.2 %copy-start.2 = (f32[8,4,1024]{2,1,0:T(4,128)S(1)}, f32[8,4,1024]{2,1,0:T(4,128)}, u32[]{:S(2)}) copy-start(f32[8,4,1024]{2,1,0:T(4,128)} %dual.1) | copy-start | bytes 393220
  0.7 1.2 %copy-start.3 = (f32[4,8,4,32]{3,2,1,0:T(4,128)S(1)}, f32[4,8,4,32]{3,2,1,0:T(4,128)}, u32[]{:S(2)}) copy-start(f32[4,8,4,32]{3,2,1,0:T(4,128)} %cons.1) | copy-start | bytes 49156
  0.7 1.2 %copy-start.4 = (f32[4,256]{1,0:T(4,128)S(1)}, f32[4,256]{1,0:T(4,128)}, u32[]{:S(2)}) copy-start(f32[4,256]{1,0:T(4,128)} %constant.2.clone.basis) | copy-start | bytes 12292
  0.7 1.2 %copy-start.5 = (s32[2,64]{1,0:T(2,128)S(1)}, s32[2,64]{1,0:T(2,128)}, u32[]{:S(2)}) copy-start(s32[2,64]{1,0:T(2,128)} %pairs.1) | copy-start | bytes 1540
  0.7 1.2 %copy-start.6 = (s32[64]{0:T(128)S(1)}, s32[64]{0:T(128)}, u32[]{:S(2)}) copy-start(s32[64]{0:T(128)} %param.10) | copy-start | bytes 772
  1.9 1.2 %copy-start = (bf16[8,64,1024]{2,1,0:T(8,128)(2,1)S(1)}, bf16[8,64,1024]{2,1,0:T(8,128)(2,1)}, u32[]{:S(2)}) copy-start(bf16[8,64,1024]{2,1,0:T(8,128)(2,1)} %coh.1) | copy-start | bytes 3145732
where the time goes:
time: 65.6 us; the launch traced here: 65.4 us
  Pallas kernels  60.3 us (92%)
  local copies, waits for them, and re-layouts  4.31 us (7%)
  between operations  0.75 us (1%)
    pallas_call x1, Pallas kernels, shards(): pl.pallas_call(kernel, out_shape=(jax.ShapeDtypeStruct(jones_field.shape,...  60.3 us
    unnamed x18, local copies, waits for them, and re-layouts  4.31 us

commit v1 on v0

--- a/solution.py
+++ b/solution.py
@@ -25,6 +25,7 @@
 ROWS = PEERS * BAND
 HEAD = 24
 GROUP = 4
+OWN = 4
 
 MESH = pl.DeviceIdType.MESH
 F32 = jnp.float32
@@ -139,56 +140,104 @@
     return jnp.dot(a, b, preferred_element_type=F32)
 
 
+def basis_at(basis, term, chan):
+    return basis[term, lax.axis_index("freq") * (CHANS // FREQS) + chan]
+
+
+def offset(group, i):
+    low, high = i % 2, i // 2
+    sign = 1 + 2 * high
+    if group == 0:
+        return 2 * (1 - low) + sign * low, sign * (1 - low) + 2 * low
+    if group == 1:
+        return 2 * low, 2 * ((low + high) % 2)
+    if group == 2:
+        return 1 + 2 * low, 1 + 2 * ((low + high) % 2)
+    return low * sign, (1 - low) * sign
+
+
 def kernel(
-    basis, coh, vis, span, pairs, jones, dual, cons,
-    jones_out, dual_out, cons_out,
-    csend, crecv, hsend, hrecv, rsend, rrecv, psend, precv,
+    basis, coh_hbm, vis_hbm, span_hbm, pairs_hbm, jones_hbm, dual_hbm, cons_hbm,
+    jones_out, lifted_out, smooth_out, rows_out,
+    coh, vis, span, pairs, jones, dual, cons,
+    perm, csend, crecv, hsend, hrecv, rsend, rrecv, psend, precv,
     meta, const, dual_t, jpq, vis_x, terms, ohg, ohs, jrhs, ones_blk, field, prior,
-    csend_sem, crecv_sem, hsend_sem, hrecv_sem, rsend_sem, rrecv_sem, psend_sem, precv_sem, own_sem,
+    csend_sem, crecv_sem, hsend_sem, hrecv_sem, rsend_sem, rrecv_sem, psend_sem, precv_sem, own_sem, in_sem,
 ):
     me = lax.axis_index("bl")
     fr = lax.axis_index("freq")
     z, y = me // RING, me % RING
-    first_chan = fr * (CHANS // FREQS)
-
-    def ahead(j):
-        return lax.rem(z + j // RING, RING) * RING + lax.rem(y + j % RING, RING)
-
-    def behind(j):
-        return lax.rem(z + RING - j // RING, RING) * RING + lax.rem(y + RING - j % RING, RING)
+
+    def ahead(group, i):
+        dz, dy = offset(group, i)
+        return lax.rem(z + dz, RING) * RING + lax.rem(y + dy, RING)
+
+    def behind(group, i):
+        dz, dy = offset(group, i)
+        return lax.rem(z + RING - dz, RING) * RING + lax.rem(y + RING - dy, RING)
+
+    def each_peer(step):
+        for group in range(4):
+            def one(i, _, group=group):
+                step(group, i)
+                return 0
+
+            lax.fori_loop(1 if group == OWN // GROUP else 0, 4, one, 0)
 
     def freq_ahead(g):
         return lax.rem(fr + g, FREQS)
 
+
+    loads = [
+        pltpu.make_async_copy(source, target, in_sem.at[i])
+        for i, (source, target) in enumerate(
+            [
+                (jones_hbm, jones), (dual_hbm, dual), (cons_hbm, cons), (vis_hbm, vis),
+                (span_hbm, span), (pairs_hbm, pairs), (coh_hbm, coh),
+            ]
+        )
+    ]
+    for load in loads:
+        load.start()
+
     barrier = pltpu.get_barrier_semaphore()
-    for j in range(1, PEERS):
-        pl.semaphore_signal(barrier, inc=1, device_id={"bl": ahead(j)}, device_id_type=MESH)
+    each_peer(
+        lambda group, i: pl.semaphore_signal(
+            barrier, inc=1, device_id={"bl": ahead(group, i)}, device_id_type=MESH
+        )
+    )
     for g in range(1, FREQS):
         pl.semaphore_signal(barrier, inc=1, device_id={"freq": freq_ahead(g)}, device_id_type=MESH)
 
-    def basis_at(term, chan):
-        return basis[term, first_chan + chan]
-
-
-    def c_copy(t, j):
+    def c_copy(t, group, i):
+        j = 4 * group + i
         return pltpu.make_async_remote_copy(
-            src_ref=csend.at[t, ahead(j)], dst_ref=crecv.at[t, j],
+            src_ref=csend.at[t, ahead(group, i)], dst_ref=crecv.at[t, j],
             send_sem=csend_sem.at[t, j], recv_sem=crecv_sem.at[t, j],
-            device_id={"bl": ahead(j)}, device_id_type=MESH,
-        )
-
-    def h_copy(t, j):
+            device_id={"bl": ahead(group, i)}, device_id_type=MESH,
+        )
+
+    def h_copy(t, group, i):
+        j = 4 * group + i
         return pltpu.make_async_remote_copy(
-            src_ref=hsend.at[t, ahead(j)], dst_ref=hrecv.at[t, j],
+            src_ref=hsend.at[t, ahead(group, i)], dst_ref=hrecv.at[t, j],
             send_sem=hsend_sem.at[t, j], recv_sem=hrecv_sem.at[t, j],
-            device_id={"bl": ahead(j)}, device_id_type=MESH,
-        )
-
-    def r_copy(t, j):
+            device_id={"bl": ahead(group, i)}, device_id_type=MESH,
+        )
+
+    def r_copy(t, group, i):
+        j = 4 * group + i
         return pltpu.make_async_remote_copy(
             src_ref=rsend.at[t, j], dst_ref=rrecv.at[t, me],
             send_sem=rsend_sem.at[t, j], recv_sem=rrecv_sem.at[t, j],
-            device_id={"bl": behind(j)}, device_id_type=MESH,
+            device_id={"bl": behind(group, i)}, device_id_type=MESH,
+        )
+
+    def arrived(t, j):
+        return pltpu.make_async_remote_copy(
+            src_ref=csend.at[t, j], dst_ref=crecv.at[t, j],
+            send_sem=csend_sem.at[t, j], recv_sem=crecv_sem.at[t, j],
+            device_id={"bl": ahead(3, 0)}, device_id_type=MESH,
         )
 
     def p_copy(g):
@@ -198,78 +247,84 @@
             device_id={"freq": freq_ahead(g)}, device_id_type=MESH,
         )
 
-
+    def own_copies(t):
+        return (
+            pltpu.make_async_copy(hsend.at[t, me], hrecv.at[t, OWN], own_sem.at[2 * t]),
+            pltpu.make_async_copy(csend.at[t, me], crecv.at[t, OWN], own_sem.at[2 * t + 1]),
+        )
+
+
+    def lanes_of(u):
+        return pl.ds(pl.multiple_of(128 * u, 128), 128)
+
+    def build_head(u, _):
+        t, tile = u // 4, u % 4
+        lanes = lanes_of(u)
+        j_tile = swap_blocks([jones[:, s, lanes] for s in range(4)])
+        d_tile = swap_blocks([dual[:, s, lanes] for s in range(4)])
+        for a in range(4):
+            d = 4 * tile + a
+            chan = 4 * u + a
+            smooth = const[0] * basis_at(basis, 0, chan)
+            for m in range(1, NTERMS):
+                smooth = smooth + const[m] * basis_at(basis, m, chan)
+            dual_t[chan] = d_tile[a]
+            hsend[t, d, 0:8, :] = j_tile[a]
+            hsend[t, d, 8:16, :] = PENALTY * smooth - d_tile[a]
+        return 0
+
+    def build_c(u, _):
+        t, tile = u // 4, u % 4
+        lanes = lanes_of(u)
+        rows = jnp.concatenate(
+            [coh[:, BAND * q : BAND * q + BAND, lanes].reshape(8 * BAND, 128) for q in range(QUARTERS)],
+            axis=1,
+        )
+        out = dot(rows, perm[...])
+        for a in range(4):
+            csend[t, 4 * tile + a] = out[:, 128 * a : 128 * a + 128].reshape(8, BAND, 128)
+        return 0
+
+    at_row = lax.broadcasted_iota(jnp.int32, (128, 128), 0)
+    apart = at_row - lax.broadcasted_iota(jnp.int32, (128, 128), 1)
+    for a in range(4):
+        for q in range(QUARTERS):
+            hit = (apart == DIRS * (a - q)) & (lax.shift_right_logical(at_row, 5) == a)
+            perm[128 * q : 128 * q + 128, 128 * a : 128 * a + 128] = jnp.where(hit, 1.0, 0.0).astype(BF16)
+
+    for load in loads[:6]:
+        load.wait()
     for m in range(NTERMS):
         for s in range(4):
             const[m, :, DIRS * s : DIRS * s + DIRS] = cons[m, :, s, :]
     meta[...] = jnp.zeros_like(meta)
     meta[0:2, 0:64] = pairs[...].astype(F32)
     meta[2:3, 0:64] = span[...].astype(F32)
-    vis_t = jnp.transpose(vis[...].reshape(8 * 64, 32))
     for t in range(STAGES):
+        for i in range(4):
+            pair = [vis[2 * i + half, PEERS * t : PEERS * t + PEERS, :] for half in range(2)]
+            hsend[t, :, 16 + i, :] = jnp.concatenate(pair, axis=1)
         for d in range(PEERS):
-            for i in range(4):
-                hsend[t, d, 16 + i : 17 + i, :] = vis_t[
-                    PEERS * t + d : PEERS * t + d + 1, 128 * i : 128 * i + 128
-                ]
             hsend[t, d, 20:24, :] = meta[0:4, :]
-
-    def build_head(t):
-        for tile in range(4):
-            lanes = pl.ds(128 * (4 * t + tile), 128)
-            j_tile = swap_blocks([jones[:, s, lanes] for s in range(4)])
-            d_tile = swap_blocks([dual[:, s, lanes] for s in range(4)])
-            for a in range(4):
-                d = 4 * tile + a
-                chan = PEERS * t + d
-                smooth = const[0] * basis_at(0, chan)
-                for m in range(1, NTERMS):
-                    smooth = smooth + const[m] * basis_at(m, chan)
-                dual_t[chan] = d_tile[a]
-                hsend[t, d, 0:8, :] = j_tile[a]
-                hsend[t, d, 8:16, :] = PENALTY * smooth - d_tile[a]
-
-    def build_c(t):
-        def one(c, _):
-            for tile in range(4):
-                lanes = pl.ds(128 * (4 * t + tile), 128)
-                parts = swap_blocks(
-                    [coh[c, BAND * q : BAND * q + BAND, lanes].astype(F32) for q in range(QUARTERS)]
-                )
-                for a in range(4):
-                    csend[t, 4 * tile + a, c] = parts[a]
-            return 0
-
-        lax.fori_loop(0, 8, one, 0)
-
-    def own_copies(t):
-        return (
-            pltpu.make_async_copy(hsend.at[t, me], hrecv.at[t, 0], own_sem.at[2 * t]),
-            pltpu.make_async_copy(csend.at[t, me], crecv.at[t, 0], own_sem.at[2 * t + 1]),
-        )
-
-    def send_all(t):
+    lax.fori_loop(0, 8, build_head, 0)
+    for load in loads[6:]:
+        load.wait()
+    lax.fori_loop(0, 4, build_c, 0)
+    pl.semaphore_wait(barrier, PEERS - 1 + FREQS - 1)
+
+    def send(t, _):
         for copy in own_copies(t):
             copy.start()
-
-        def head(j, _):
-            h_copy(t, j).start()
-            return 0
-
-        def body(j, _):
-            c_copy(t, j).start()
-            return 0
-
-        lax.fori_loop(1, PEERS, head, 0)
-        lax.fori_loop(1, PEERS, body, 0)
-
-    build_head(0)
-    build_c(0)
-    pl.semaphore_wait(barrier, PEERS - 1 + FREQS - 1)
-    send_all(0)
-    build_head(1)
-    build_c(1)
-    send_all(1)
+        each_peer(lambda group, i: h_copy(t, group, i).start())
+        each_peer(lambda group, i: c_copy(t, group, i).start())
+
+        @pl.when(t == 0)
+        def _():
+            lax.fori_loop(4, 8, build_c, 0)
+
+        return 0
+
+    lax.fori_loop(0, STAGES, send, 0)
 
     row_block = lax.shift_right_logical(lax.broadcasted_iota(jnp.int32, (256, 128), 0), 5) & 3
     ones_blk[...] = jnp.where(row_block == lane_block((256, 128)), 1.0, 0.0).astype(BF16)
@@ -295,8 +350,14 @@
         ).astype(BF16)
         position = lax.broadcasted_iota(jnp.int32, (1, 256), 1) & (SLOTS - 1)
         j = position & (PEERS - 1)
-        owner_z = (z + RING - lax.shift_right_logical(j, 2)) & (RING - 1)
-        owner_y = (y + RING - (j & 3)) & (RING - 1)
+        dz, dy = offset(0, j & 3)
+        for group in range(1, 4):
+            group_z, group_y = offset(group, j & 3)
+            inside = lax.shift_right_logical(j, 2) == group
+            dz = jnp.where(inside, group_z, dz)
+            dy = jnp.where(inside, group_y, dy)
+        owner_z = (z + RING - dz) & (RING - 1)
+        owner_y = (y + RING - dy) & (RING - 1)
         label = 4 * (owner_z * RING + owner_y) + lax.shift_right_logical(position, 4)
         label = label.astype(F32)
         weight = dot(banded(0, 22).astype(BF16), expand)
@@ -401,109 +462,155 @@
                 flat = jnp.where(block == s, whole[PEERS * s : PEERS * s + PEERS], flat)
             for j in range(PEERS):
                 rsend[t, j, c : c + 1, :] = flat[j : j + 1]
-        rrecv[t, me] = rsend[t, 0]
-        for j in range(1, PEERS):
-            r_copy(t, j).start()
-
-    def wait_each(copy, t):
-        def one(j, _):
-            copy(t, j).wait()
-            return 0
-
-        lax.fori_loop(1, PEERS, one, 0)
-
-    for t in range(STAGES):
+        rrecv[t, me] = rsend[t, OWN]
+        each_peer(lambda group, i: r_copy(t, group, i).start())
+
+    def stage(t, _):
         own = own_copies(t)
         own[0].wait()
-        wait_each(h_copy, t)
-        if t == 0:
+        each_peer(lambda group, i: h_copy(t, group, i).wait_recv())
+
+        @pl.when(t == 0)
+        def _():
             build_onehots()
+
         build_visibility(t)
         build_field(t)
-        gather()
         own[1].wait()
 
-        def first_sweep(group, _):
-            def arrive(j, _):
-                c_copy(t, j).wait()
+        def sweep(i, _):
+            gather()
+
+            def one_group(group, _):
+                for source in range(4):
+                    @pl.when((i == 0) & (group * 4 + source != OWN))
+                    def _():
+                        arrived(t, group * 4 + source).wait_recv()
+
+                process(t, group)
                 return 0
 
-            lax.fori_loop(jnp.maximum(group * GROUP, 1), (group + 1) * GROUP, arrive, 0)
-            process(t, group)
+            lax.fori_loop(0, PEERS // GROUP, one_group, 0)
+            solve()
             return 0
 
-        def later_sweep(group, _):
-            process(t, group)
-            return 0
-
-        lax.fori_loop(0, PEERS // GROUP, first_sweep, 0)
-        solve()
-        for _ in range(1, ITERS):
-            gather()
-            lax.fori_loop(0, PEERS // GROUP, later_sweep, 0)
-            solve()
+        lax.fori_loop(0, ITERS, sweep, 0)
         send_back(t)
-
-    projected = [jnp.zeros((8, 128), F32) for _ in range(NTERMS)]
-    for t in range(STAGES):
-        wait_each(r_copy, t)
-        for d in range(PEERS):
+        return 0
+
+    lax.fori_loop(0, STAGES, stage, 0)
+
+    def project(t, projected):
+        each_peer(lambda group, i: r_copy(t, group, i).wait_recv())
+
+        def one(d, projected):
             chan = PEERS * t + d
             blended = rrecv[t, d] + dual_t[chan] * (1.0 / PENALTY)
-            for m in range(NTERMS):
-                projected[m] = projected[m] + blended * (basis_at(m, chan) * (1.0 / norm_of(m)))
+            return tuple(
+                projected[m] + blended * (basis_at(basis, m, chan) * (1.0 / norm_of(m)))
+                for m in range(NTERMS)
+            )
+
+        return lax.fori_loop(0, PEERS, one, projected)
+
+    lane = lane_block((1, 128))
+
+    def basis_rows(u, _):
+        for m in range(NTERMS):
+            row = jnp.full((1, 128), basis_at(basis, m, 4 * u), F32)
+            for a in range(1, 4):
+                row = jnp.where(lane == a, basis_at(basis, m, 4 * u + a), row)
+            rows_out[m : m + 1, lanes_of(u)] = PENALTY * row
+        return 0
+
+    def finish(u, _):
+        lanes = lanes_of(u)
+        t, tile = u // 4, u % 4
+        parts = swap_blocks([rrecv[t, 4 * tile + a] for a in range(4)])
+        for s in range(4):
+            jones_out[:, s, lanes] = parts[s]
+            lifted_out[:, s, lanes] = dual[:, s, lanes] + PENALTY * parts[s]
+        return 0
+
+    def sent(t, _):
+        for copy in (h_copy, c_copy):
+            each_peer(lambda group, i, copy=copy: copy(t, group, i).wait_send())
+        return 0
+
+    projected = project(0, tuple(jnp.zeros((8, 128), F32) for _ in range(NTERMS)))
+    lax.fori_loop(0, 8, basis_rows, 0)
+    lax.fori_loop(0, 4, finish, 0)
+    lax.fori_loop(0, STAGES, sent, 0)
+    projected = project(1, projected)
     for m in range(NTERMS):
         psend[m] = projected[m]
         precv[fr, m] = projected[m]
-    for g in range(1, FREQS):
+    for g in (4, 5, 3, 6, 2, 7, 1):
         p_copy(g).start()
+    lax.fori_loop(4, 8, finish, 0)
     for t in range(STAGES):
-        for tile in range(4):
-            lanes = pl.ds(128 * (4 * t + tile), 128)
-            parts = swap_blocks([rrecv[t, 4 * tile + a] for a in range(4)])
-            for s in range(4):
-                jones_out[:, s, lanes] = parts[s]
+        each_peer(lambda group, i, t=t: r_copy(t, group, i).wait_send())
     for g in range(1, FREQS):
         p_copy(g).wait()
     block = lane_block((8, 128))
-    smooth = []
     for m in range(NTERMS):
         total = precv[0, m]
         for g in range(1, FREQS):
             total = total + precv[g, m]
         for s in range(4):
-            cons_out[m, :, s, :] = total[:, DIRS * s : DIRS * s + DIRS]
-        smooth.append([spread_lanes(jnp.where(block == s, total, 0.0)) for s in range(4)])
-    lane = lane_block((1, 128))
+            smooth_out[m, :, s, :] = spread_lanes(jnp.where(block == s, total, 0.0))
+
+
+def finish_kernel(jones, lifted, smooth, rows, jones_out, dual_hbm, cons_hbm, dual_out, cons_out, sem):
+    copy = pltpu.make_async_copy(jones, jones_out, sem.at[0])
+    copy.start()
+    for m in range(NTERMS):
+        cons_out[m] = smooth[m, :, :, 0:DIRS]
+    cons_copy = pltpu.make_async_copy(cons_out, cons_hbm, sem.at[1])
+    cons_copy.start()
     for tile in range(8):
-        lanes = pl.ds(128 * tile, 128)
-        rows = []
-        for m in range(NTERMS):
-            row = jnp.full((1, 128), basis_at(m, 4 * tile), F32)
-            for a in range(1, 4):
-                row = jnp.where(lane == a, basis_at(m, 4 * tile + a), row)
-            rows.append(row)
-        for s in range(4):
-            fitted = rows[0] * smooth[0][s]
+        lanes = slice(128 * tile, 128 * tile + 128)
+        scale = [jnp.broadcast_to(rows[m : m + 1, lanes], (4, 128)) for m in range(NTERMS)]
+        for c in range(8):
+            fitted = scale[0] * smooth[0, c]
             for m in range(1, NTERMS):
-                fitted = fitted + rows[m] * smooth[m][s]
-            dual_out[:, s, lanes] = dual[:, s, lanes] + PENALTY * (jones_out[:, s, lanes] - fitted)
+                fitted = fitted + scale[m] * smooth[m, c]
+            dual_out[c, :, lanes] = lifted[c, :, lanes] - fitted
+    dual_copy = pltpu.make_async_copy(dual_out, dual_hbm, sem.at[2])
+    dual_copy.start()
+    copy.wait()
+    cons_copy.wait()
+    dual_copy.wait()
 
 
 def shards(coherency, visibility, span_lengths, station_pairs, jones_field, dual_field, consensus):
     vmem = pl.BlockSpec(memory_space=pltpu.VMEM)
     smem = pl.BlockSpec(memory_space=pltpu.SMEM)
+    hbm = pl.BlockSpec(memory_space=pltpu.HBM)
     dma = pltpu.SemaphoreType.DMA
-    return pl.pallas_call(
+    basis = jnp.asarray(basis_table())
+    operands = (
+        coherency,
+        jnp.transpose(visibility, (0, 2, 1)),
+        span_lengths.reshape(1, -1),
+        station_pairs,
+        jones_field,
+        dual_field,
+        consensus,
+    )
+    jones, lifted, smooth, rows = pl.pallas_call(
         kernel,
         out_shape=(
             jax.ShapeDtypeStruct(jones_field.shape, F32),
             jax.ShapeDtypeStruct(dual_field.shape, F32),
-            jax.ShapeDtypeStruct(consensus.shape, F32),
+            jax.ShapeDtypeStruct((NTERMS, 8, 4, 128), F32),
+            jax.ShapeDtypeStruct((NTERMS, jones_field.shape[2]), F32),
         ),
-        in_specs=[smem] + [vmem] * 7,
-        out_specs=(vmem,) * 3,
-        scratch_shapes=[
+        in_specs=[smem] + [hbm] * 7,
+        out_specs=(vmem,) * 4,
+        scratch_shapes=[pltpu.VMEM(x.shape, x.dtype) for x in operands]
+        + [
+            pltpu.VMEM((512, 512), BF16),
             pltpu.VMEM((STAGES, PEERS, 8, BAND, 128), F32),
             pltpu.VMEM((STAGES, PEERS, 8, BAND, 128), F32),
             pltpu.VMEM((STAGES, PEERS, HEAD, 128), F32),
@@ -533,21 +640,25 @@
             dma((FREQS,)),
             dma((FREQS,)),
             dma((2 * STAGES,)),
+            dma((7,)),
         ],
         compiler_params=pltpu.CompilerParams(
-            collective_id=0, has_side_effects=True, vmem_limit_bytes=40 * 2**20
+            collective_id=0, has_side_effects=True, vmem_limit_bytes=60 * 2**20
         ),
         name="calibrate",
-    )(
-        jnp.asarray(basis_table()),
-        coherency,
-        visibility,
-        span_lengths.reshape(1, -1),
-        station_pairs,
-        jones_field,
-        dual_field,
-        consensus,
-    )
+    )(basis, *operands)
+    return pl.pallas_call(
+        finish_kernel,
+        out_shape=(
+            jax.ShapeDtypeStruct(jones_field.shape, F32),
+            jax.ShapeDtypeStruct(dual_field.shape, F32),
+            jax.ShapeDtypeStruct(consensus.shape, F32),
+        ),
+        in_specs=[vmem] * 4,
+        out_specs=(hbm, hbm, hbm),
+        scratch_shapes=[pltpu.VMEM(dual_field.shape, F32), pltpu.VMEM(consensus.shape, F32), dma((3,))],
+        name="finish",
+    )(jones, lifted, smooth, rows)
 
 
 def solution(mesh):

time: 65.6 us -> 64.9 us (0.989)
  local copies, waits for them, and re-layouts: 4.31 us -> 0 us
  Pallas kernels: 60.3 us -> 64.1 us
    unnamed x18 -> x0, local copies, waits for them, and re-layouts: 4.31 us -> none
    pallas_call x1, Pallas kernels: 60.3 us -> 62.4 us  [shards(): pl.pallas_call(kernel, out_shape=(jax.ShapeDtypeStruct(jones_field.shape,...]
    pallas_call x0 -> x1, Pallas kernels: none -> 1.74 us  [shards(): pl.pallas_call(finish_kernel, out_shape=(jax.ShapeDtypeStruct(jones_field...]
where the time goes in v1:
time: 64.9 us; the launch traced here: 64.8 us
  Pallas kernels  64.1 us (99%)
    pallas_call x1, Pallas kernels, shards(): pl.pallas_call(kernel, out_shape=(jax.ShapeDtypeStruct(jones_field.shape,...  62.4 us
    pallas_call x1, Pallas kernels, shards(): pl.pallas_call(finish_kernel, out_shape=(jax.ShapeDtypeStruct(jones_field...  1.74 us

profile of v1, /device:TPU:1, one launch (start us, length us, event | category | flops | bytes accessed | tf_op | source)
XLA Modules:
  0.0 64.8 jit_solution(14192354880033050240)
XLA Ops:
  0.6 62.4 %calibrate.1 = (f32[8,4,1024]{2,1,0:T(4,128)}, f32[8,4,1024]{2,1,0:T(4,128)}, f32[4,8,4,128]{3,2,1,0:T(4,128)}, f32[4,1024]{1,0:T(4,128)}) custom-call(f32[4,256]{1,0:T(4,128)} %constant.2.clone.basis, bf16[8,64,1024]{2,1,0:T(8,128)(2,1)} %coh_hbm.1, f32[8,32,64]{2,1,0:T(8,128)} %bitcast.2, s32[1,64]{1,0:T(1,128)} %bitcast.3, s32[2,64]{1,0:T(2,128)} %pairs_hbm.1, ...), custom_call_target="tpu_custom_call" | custom-call | tf_op jit(solution)/shard_map/calibrate/pallas_call | solution.py:601
  63.0 1.7 %finish.1 = (f32[8,4,1024]{2,1,0:T(4,128)}, f32[8,4,1024]{2,1,0:T(4,128)}, f32[4,8,4,32]{3,2,1,0:T(4,128)}) custom-call(f32[8,4,1024]{2,1,0:T(4,128)} %get-tuple-element.7.jones, f32[8,4,1024]{2,1,0:T(4,128)} %get-tuple-element.8.lifted, f32[4,8,4,128]{3,2,1,0:T(4,128)} %get-tuple-element.9.smooth, f32[4,1024]{1,0:T(4,128)} %get-tuple-element.10.rows), custom_call_target="tpu_custom_call" | custom-call | tf_op jit(solution)/shard_map/finish/pallas_call | solution.py:650

commit v2 on v1

--- a/solution.py
+++ b/solution.py
@@ -23,7 +23,7 @@
 DIRS = 32
 SLOTS = 64
 ROWS = PEERS * BAND
-HEAD = 24
+HEAD = 16
 GROUP = 4
 OWN = 4
 
@@ -162,7 +162,7 @@
     coh, vis, span, pairs, jones, dual, cons,
     perm, csend, crecv, hsend, hrecv, rsend, rrecv, psend, precv,
     meta, const, dual_t, jpq, vis_x, terms, ohg, ohs, jrhs, ones_blk, field, prior,
-    csend_sem, crecv_sem, hsend_sem, hrecv_sem, rsend_sem, rrecv_sem, psend_sem, precv_sem, own_sem, in_sem,
+    csend_sem, crecv_sem, hsend_sem, hrecv_sem, rsend_sem, rrecv_sem, psend_sem, precv_sem, own_sem, in_sem, qsend_sem, qrecv_sem,
 ):
     me = lax.axis_index("bl")
     fr = lax.axis_index("freq")
@@ -220,8 +220,16 @@
     def h_copy(t, group, i):
         j = 4 * group + i
         return pltpu.make_async_remote_copy(
-            src_ref=hsend.at[t, ahead(group, i)], dst_ref=hrecv.at[t, j],
+            src_ref=hsend.at[t, ahead(group, i), pl.ds(0, HEAD)], dst_ref=hrecv.at[t, j, pl.ds(0, HEAD)],
             send_sem=hsend_sem.at[t, j], recv_sem=hrecv_sem.at[t, j],
+            device_id={"bl": ahead(group, i)}, device_id_type=MESH,
+        )
+
+    def q_copy(t, group, i):
+        j = 4 * group + i
+        return pltpu.make_async_remote_copy(
+            src_ref=hsend.at[t, ahead(group, i), pl.ds(HEAD, 8)], dst_ref=hrecv.at[t, j, pl.ds(HEAD, 8)],
+            send_sem=qsend_sem.at[t, j], recv_sem=qrecv_sem.at[t, j],
             device_id={"bl": ahead(group, i)}, device_id_type=MESH,
         )
 
@@ -270,7 +278,7 @@
                 smooth = smooth + const[m] * basis_at(basis, m, chan)
             dual_t[chan] = d_tile[a]
             hsend[t, d, 0:8, :] = j_tile[a]
-            hsend[t, d, 8:16, :] = PENALTY * smooth - d_tile[a]
+            hsend[t, d, 16:24, :] = PENALTY * smooth - d_tile[a]
         return 0
 
     def build_c(u, _):
@@ -303,9 +311,9 @@
     for t in range(STAGES):
         for i in range(4):
             pair = [vis[2 * i + half, PEERS * t : PEERS * t + PEERS, :] for half in range(2)]
-            hsend[t, :, 16 + i, :] = jnp.concatenate(pair, axis=1)
+            hsend[t, :, 8 + i, :] = jnp.concatenate(pair, axis=1)
         for d in range(PEERS):
-            hsend[t, d, 20:24, :] = meta[0:4, :]
+            hsend[t, d, 12:16, :] = meta[0:4, :]
     lax.fori_loop(0, 8, build_head, 0)
     for load in loads[6:]:
         load.wait()
@@ -317,6 +325,7 @@
             copy.start()
         each_peer(lambda group, i: h_copy(t, group, i).start())
         each_peer(lambda group, i: c_copy(t, group, i).start())
+        each_peer(lambda group, i: q_copy(t, group, i).start())
 
         @pl.when(t == 0)
         def _():
@@ -360,9 +369,9 @@
         owner_y = (y + RING - dy) & (RING - 1)
         label = 4 * (owner_z * RING + owner_y) + lax.shift_right_logical(position, 4)
         label = label.astype(F32)
-        weight = dot(banded(0, 22).astype(BF16), expand)
+        weight = dot(banded(0, 14).astype(BF16), expand)
         for side in range(2):
-            station = dot(banded(0, 20 + side).astype(BF16), expand)
+            station = dot(banded(0, 12 + side).astype(BF16), expand)
             hit = station == label
             onehot = jnp.where(hit, 1.0, 0.0).astype(BF16)
             ohg[ROWS * side : ROWS * side + ROWS, 0:256] = onehot
@@ -378,18 +387,19 @@
             lax.shift_right_logical(source, 4) == lax.shift_right_logical(target, 5), 1.0, 0.0
         ).astype(BF16)
         for i in range(4):
-            high, low = halves(banded(t, 16 + i))
+            high, low = halves(banded(t, 8 + i))
             out = dot(jnp.concatenate([high, low], axis=1), expand)
             vis_x[2 * i] = out[:, 0:128]
             vis_x[2 * i + 1] = out[:, 128:256]
 
-    def build_field(t):
+    def unpack(t, first, target):
         block = lane_block((PEERS, 128))
-        for c in range(16):
-            flat = jnp.concatenate([hrecv[t, j, c : c + 1, :] for j in range(PEERS)], axis=0)
-            target = field if c < 8 else prior
+        for c in range(8):
+            flat = jnp.concatenate(
+                [hrecv[t, j, first + c : first + c + 1, :] for j in range(PEERS)], axis=0
+            )
             for s in range(4):
-                target[c % 8, PEERS * s : PEERS * s + PEERS] = spread_lanes(
+                target[c, PEERS * s : PEERS * s + PEERS] = spread_lanes(
                     jnp.where(block == s, flat, 0.0)
                 )
 
@@ -475,7 +485,7 @@
             build_onehots()
 
         build_visibility(t)
-        build_field(t)
+        unpack(t, 0, field)
         own[1].wait()
 
         def sweep(i, _):
@@ -491,6 +501,11 @@
                 return 0
 
             lax.fori_loop(0, PEERS // GROUP, one_group, 0)
+            @pl.when(i == 0)
+            def _():
+                each_peer(lambda group, i: q_copy(t, group, i).wait_recv())
+                unpack(t, HEAD, prior)
+
             solve()
             return 0
 
@@ -533,7 +548,7 @@
         return 0
 
     def sent(t, _):
-        for copy in (h_copy, c_copy):
+        for copy in (h_copy, q_copy, c_copy):
             each_peer(lambda group, i, copy=copy: copy(t, group, i).wait_send())
         return 0
 
@@ -613,8 +628,8 @@
             pltpu.VMEM((512, 512), BF16),
             pltpu.VMEM((STAGES, PEERS, 8, BAND, 128), F32),
             pltpu.VMEM((STAGES, PEERS, 8, BAND, 128), F32),
-            pltpu.VMEM((STAGES, PEERS, HEAD, 128), F32),
-            pltpu.VMEM((STAGES, PEERS, HEAD, 128), F32),
+            pltpu.VMEM((STAGES, PEERS, HEAD + 8, 128), F32),
+            pltpu.VMEM((STAGES, PEERS, HEAD + 8, 128), F32),
             pltpu.VMEM((STAGES, PEERS, 8, 128), F32),
             pltpu.VMEM((STAGES, PEERS, 8, 128), F32),
             pltpu.VMEM((NTERMS, 8, 128), F32),
@@ -641,6 +656,8 @@
             dma((FREQS,)),
             dma((2 * STAGES,)),
             dma((7,)),
+            dma((STAGES, PEERS)),
+            dma((STAGES, PEERS)),
         ],
         compiler_params=pltpu.CompilerParams(
             collective_id=0, has_side_effects=True, vmem_limit_bytes=60 * 2**20

time: 64.9 us -> 62.1 us (0.957)
  Pallas kernels: 64.1 us -> 61.3 us
    pallas_call x1, Pallas kernels: 62.4 us -> 59.5 us  [shards(): pl.pallas_call(kernel, out_shape=(jax.ShapeDtypeStruct(jones_field.shape,...]
where the time goes in v2:
time: 62.1 us; the launch traced here: 61.9 us
  Pallas kernels  61.3 us (99%)
  between operations  0.64 us (1%)
    pallas_call x1, Pallas kernels, shards(): pl.pallas_call(kernel, out_shape=(jax.ShapeDtypeStruct(jones_field.shape,...  59.5 us
    pallas_call x1, Pallas kernels, shards(): pl.pallas_call(finish_kernel, out_shape=(jax.ShapeDtypeStruct(jones_field...  1.74 us

profile of v2, /device:TPU:1, one launch (start us, length us, event | category | flops | bytes accessed | tf_op | source)
XLA Modules:
  0.0 61.9 jit_solution(12350663416621909106)
XLA Ops:
  0.6 59.5 %calibrate.1 = (f32[8,4,1024]{2,1,0:T(4,128)}, f32[8,4,1024]{2,1,0:T(4,128)}, f32[4,8,4,128]{3,2,1,0:T(4,128)}, f32[4,1024]{1,0:T(4,128)}) custom-call(f32[4,256]{1,0:T(4,128)} %constant.2.clone.basis, bf16[8,64,1024]{2,1,0:T(8,128)(2,1)} %coh_hbm.1, f32[8,32,64]{2,1,0:T(8,128)} %bitcast.2, s32[1,64]{1,0:T(1,128)} %bitcast.3, s32[2,64]{1,0:T(2,128)} %pairs_hbm.1, ...), custom_call_target="tpu_custom_call" | custom-call | tf_op jit(solution)/shard_map/calibrate/pallas_call | solution.py:616
  60.2 1.7 %finish.1 = (f32[8,4,1024]{2,1,0:T(4,128)}, f32[8,4,1024]{2,1,0:T(4,128)}, f32[4,8,4,32]{3,2,1,0:T(4,128)}) custom-call(f32[8,4,1024]{2,1,0:T(4,128)} %get-tuple-element.7.jones, f32[8,4,1024]{2,1,0:T(4,128)} %get-tuple-element.8.lifted, f32[4,8,4,128]{3,2,1,0:T(4,128)} %get-tuple-element.9.smooth, f32[4,1024]{1,0:T(4,128)} %get-tuple-element.10.rows), custom_call_target="tpu_custom_call" | custom-call | tf_op jit(solution)/shard_map/finish/pallas_call | solution.py:667

commit v3 on v2

--- a/solution.py
+++ b/solution.py
@@ -308,32 +308,28 @@
     meta[...] = jnp.zeros_like(meta)
     meta[0:2, 0:64] = pairs[...].astype(F32)
     meta[2:3, 0:64] = span[...].astype(F32)
-    for t in range(STAGES):
+    def build_heads(t):
         for i in range(4):
             pair = [vis[2 * i + half, PEERS * t : PEERS * t + PEERS, :] for half in range(2)]
             hsend[t, :, 8 + i, :] = jnp.concatenate(pair, axis=1)
         for d in range(PEERS):
             hsend[t, d, 12:16, :] = meta[0:4, :]
-    lax.fori_loop(0, 8, build_head, 0)
-    for load in loads[6:]:
-        load.wait()
-    lax.fori_loop(0, 4, build_c, 0)
+        lax.fori_loop(4 * t, 4 * t + 4, build_head, 0)
+
+    build_heads(0)
     pl.semaphore_wait(barrier, PEERS - 1 + FREQS - 1)
-
-    def send(t, _):
-        for copy in own_copies(t):
-            copy.start()
-        each_peer(lambda group, i: h_copy(t, group, i).start())
-        each_peer(lambda group, i: c_copy(t, group, i).start())
-        each_peer(lambda group, i: q_copy(t, group, i).start())
-
-        @pl.when(t == 0)
-        def _():
-            lax.fori_loop(4, 8, build_c, 0)
-
-        return 0
-
-    lax.fori_loop(0, STAGES, send, 0)
+    for t in range(STAGES):
+        if t > 0:
+            build_heads(t)
+        own_copies(t)[0].start()
+        each_peer(lambda group, i, t=t: h_copy(t, group, i).start())
+        if t == 0:
+            for load in loads[6:]:
+                load.wait()
+        lax.fori_loop(4 * t, 4 * t + 4, build_c, 0)
+        own_copies(t)[1].start()
+        each_peer(lambda group, i, t=t: c_copy(t, group, i).start())
+        each_peer(lambda group, i, t=t: q_copy(t, group, i).start())
 
     row_block = lax.shift_right_logical(lax.broadcasted_iota(jnp.int32, (256, 128), 0), 5) & 3
     ones_blk[...] = jnp.where(row_block == lane_block((256, 128)), 1.0, 0.0).astype(BF16)

time: 62.1 us -> 61.5 us (level)
  Pallas kernels: 61.3 us -> 60.6 us
    pallas_call x1, Pallas kernels: 59.5 us -> 58.9 us  [shards(): pl.pallas_call(kernel, out_shape=(jax.ShapeDtypeStruct(jones_field.shape,...]
where the time goes in v3:
time: 61.5 us; the launch traced here: 61.3 us
  Pallas kernels  60.6 us (99%)
  between operations  0.64 us (1%)
    pallas_call x1, Pallas kernels, shards(): pl.pallas_call(kernel, out_shape=(jax.ShapeDtypeStruct(jones_field.shape,...  58.9 us
    pallas_call x1, Pallas kernels, shards(): pl.pallas_call(finish_kernel, out_shape=(jax.ShapeDtypeStruct(jones_field...  1.74 us

profile of v3, /device:TPU:1, one launch (start us, length us, event | category | flops | bytes accessed | tf_op | source)
XLA Modules:
  0.0 61.3 jit_solution(13895847431754021227)
XLA Ops:
  0.6 58.9 %calibrate.1 = (f32[8,4,1024]{2,1,0:T(4,128)}, f32[8,4,1024]{2,1,0:T(4,128)}, f32[4,8,4,128]{3,2,1,0:T(4,128)}, f32[4,1024]{1,0:T(4,128)}) custom-call(f32[4,256]{1,0:T(4,128)} %constant.2.clone.basis, bf16[8,64,1024]{2,1,0:T(8,128)(2,1)} %coh_hbm.1, f32[8,32,64]{2,1,0:T(8,128)} %bitcast.2, s32[1,64]{1,0:T(1,128)} %bitcast.3, s32[2,64]{1,0:T(2,128)} %pairs_hbm.1, ...), custom_call_target="tpu_custom_call" | custom-call | tf_op jit(solution)/shard_map/calibrate/pallas_call | solution.py:612
  59.5 1.7 %finish.1 = (f32[8,4,1024]{2,1,0:T(4,128)}, f32[8,4,1024]{2,1,0:T(4,128)}, f32[4,8,4,32]{3,2,1,0:T(4,128)}) custom-call(f32[8,4,1024]{2,1,0:T(4,128)} %get-tuple-element.7.jones, f32[8,4,1024]{2,1,0:T(4,128)} %get-tuple-element.8.lifted, f32[4,8,4,128]{3,2,1,0:T(4,128)} %get-tuple-element.9.smooth, f32[4,1024]{1,0:T(4,128)} %get-tuple-element.10.rows), custom_call_target="tpu_custom_call" | custom-call | tf_op jit(solution)/shard_map/finish/pallas_call | solution.py:663

commit v4 on v3

--- a/solution.py
+++ b/solution.py
@@ -176,13 +176,18 @@
         dz, dy = offset(group, i)
         return lax.rem(z + RING - dz, RING) * RING + lax.rem(y + RING - dy, RING)
 
-    def each_peer(step):
+    def each_peer(step, unroll=False):
         for group in range(4):
             def one(i, _, group=group):
                 step(group, i)
                 return 0
 
-            lax.fori_loop(1 if group == OWN // GROUP else 0, 4, one, 0)
+            first = 1 if group == OWN // GROUP else 0
+            if unroll:
+                for i in range(first, 4):
+                    step(group, i)
+            else:
+                lax.fori_loop(first, 4, one, 0)
 
     def freq_ahead(g):
         return lax.rem(fr + g, FREQS)
@@ -204,7 +209,8 @@
     each_peer(
         lambda group, i: pl.semaphore_signal(
             barrier, inc=1, device_id={"bl": ahead(group, i)}, device_id_type=MESH
-        )
+        ),
+        unroll=True,
     )
     for g in range(1, FREQS):
         pl.semaphore_signal(barrier, inc=1, device_id={"freq": freq_ahead(g)}, device_id_type=MESH)
@@ -322,13 +328,13 @@
         if t > 0:
             build_heads(t)
         own_copies(t)[0].start()
-        each_peer(lambda group, i, t=t: h_copy(t, group, i).start())
+        each_peer(lambda group, i, t=t: h_copy(t, group, i).start(), unroll=True)
         if t == 0:
             for load in loads[6:]:
                 load.wait()
         lax.fori_loop(4 * t, 4 * t + 4, build_c, 0)
         own_copies(t)[1].start()
-        each_peer(lambda group, i, t=t: c_copy(t, group, i).start())
+        each_peer(lambda group, i, t=t: c_copy(t, group, i).start(), unroll=True)
         each_peer(lambda group, i, t=t: q_copy(t, group, i).start())
 
     row_block = lax.shift_right_logical(lax.broadcasted_iota(jnp.int32, (256, 128), 0), 5) & 3
@@ -469,7 +475,7 @@
             for j in range(PEERS):
                 rsend[t, j, c : c + 1, :] = flat[j : j + 1]
         rrecv[t, me] = rsend[t, OWN]
-        each_peer(lambda group, i: r_copy(t, group, i).start())
+        each_peer(lambda group, i: r_copy(t, group, i).start(), unroll=True)
 
     def stage(t, _):
         own = own_copies(t)

time: 61.5 us -> 61.5 us (level)
  no operation moved by 1% of the time
where the time goes in v4:
time: 61.5 us; the launch traced here: 61.3 us
  Pallas kernels  60.7 us (99%)
  between operations  0.64 us (1%)
    pallas_call x1, Pallas kernels, shards(): pl.pallas_call(kernel, out_shape=(jax.ShapeDtypeStruct(jones_field.shape,...  59 us
    pallas_call x1, Pallas kernels, shards(): pl.pallas_call(finish_kernel, out_shape=(jax.ShapeDtypeStruct(jones_field...  1.74 us

profile of v4, /device:TPU:1, one launch (start us, length us, event | category | flops | bytes accessed | tf_op | source)
XLA Modules:
  0.0 61.3 jit_solution(9809005379953907938)
XLA Ops:
  0.6 59.0 %calibrate.1 = (f32[8,4,1024]{2,1,0:T(4,128)}, f32[8,4,1024]{2,1,0:T(4,128)}, f32[4,8,4,128]{3,2,1,0:T(4,128)}, f32[4,1024]{1,0:T(4,128)}) custom-call(f32[4,256]{1,0:T(4,128)} %constant.2.clone.basis, bf16[8,64,1024]{2,1,0:T(8,128)(2,1)} %coh_hbm.1, f32[8,32,64]{2,1,0:T(8,128)} %bitcast.2, s32[1,64]{1,0:T(1,128)} %bitcast.3, s32[2,64]{1,0:T(2,128)} %pairs_hbm.1, ...), custom_call_target="tpu_custom_call" | custom-call | tf_op jit(solution)/shard_map/calibrate/pallas_call | solution.py:618
  59.6 1.7 %finish.1 = (f32[8,4,1024]{2,1,0:T(4,128)}, f32[8,4,1024]{2,1,0:T(4,128)}, f32[4,8,4,32]{3,2,1,0:T(4,128)}) custom-call(f32[8,4,1024]{2,1,0:T(4,128)} %get-tuple-element.7.jones, f32[8,4,1024]{2,1,0:T(4,128)} %get-tuple-element.8.lifted, f32[4,8,4,128]{3,2,1,0:T(4,128)} %get-tuple-element.9.smooth, f32[4,1024]{1,0:T(4,128)} %get-tuple-element.10.rows), custom_call_target="tpu_custom_call" | custom-call | tf_op jit(solution)/shard_map/finish/pallas_call | solution.py:669
